TPU v7x, 32 devices: a whole 2x2x4 slice. The times are simulated.
32 devices in a mesh: leaf: 8 (over y, x, core), rhs: 4 (over z).
Axes of the slice: x: 2, y: 2, z: 4, core: 2. Of those that a mesh axis runs over, the one named last changes fastest.
Arguments:
- rhs_cols: bfloat16 [65536, 512], P('leaf', 'rhs'), may hold values from -6 to 6
- leaf_inv: bfloat16 [128, 512, 512], P('leaf', 'rhs')
- leaf_basis: bfloat16 [128, 512, 128], P('leaf'), may hold values from -0.25 to 0.25
- leaf_back: bfloat16 [128, 512, 128], P('leaf'), may hold values from -0.5 to 0.5
- leaf_coarse: float32 [128, 128, 128], P('leaf')
- mid_inv: float32 [120, 256, 256], P('leaf')
- mid_basis: float32 [120, 256, 128], P('leaf'), may hold values from -0.375 to 0.375
- mid_back: float32 [120, 256, 128], P('leaf'), may hold values from -0.5 to 0.5
- mid_coarse: float32 [120, 128, 128], P('leaf')
- top_inv: float32 [8, 256, 256], P('leaf')
- top_basis: float32 [8, 256, 128], P('leaf'), may hold values from -0.375 to 0.375
- top_back: float32 [8, 256, 128], P('leaf'), may hold values from -0.5 to 0.5
- top_coarse: float32 [8, 128, 128], P('leaf')
Outputs:
- solution: float32 [65536, 512], P('leaf', 'rhs')
All inputs are finite; a program needn't handle non-finite values.
Results may differ from a plain program's by a relative error of at most 0.004.
Values may be sent and summed in bfloat16 or wider, within the bound.
A program may use at most 192 MiB of HBM per device.

v0:
```python
import jax
import jax.numpy as jnp
from jax import lax
from jax.sharding import PartitionSpec as P

exact_mode = lax.Precision.HIGHEST


def swapped(array, axis, bit):
    return lax.ppermute(array, axis, [(i, i ^ 1 << bit) for i in range(lax.axis_size(axis))])


def node_up(inverse, basis_mat, coarse, stacked):
    solved = jnp.einsum("nij,njc->nic", inverse, stacked, precision=exact_mode)
    reduced = jnp.einsum("nik,nic->nkc", basis_mat, solved, precision=exact_mode)
    upward = jnp.einsum("nkl,nlc->nkc", coarse, reduced, precision=exact_mode)
    return (solved, reduced, upward)


def node_down(solved, reduced, back_mat, parent_part):
    return solved - jnp.einsum(
        "nik,nkc->nic", back_mat, reduced - parent_part, precision=exact_mode
    )


def top_doubling(current, every_inv, every_basis, every_back, every_coarse, tree_depth, position):
    basis_rank = current.shape[1]
    stored = []
    for height in range(1, tree_depth + 1):
        level_bit = height - 1
        partner = swapped(current, "leaf", level_bit)
        is_left = (position >> level_bit) % 2 == 0
        left_part = jnp.where(is_left, current, partner)
        right_part = jnp.where(is_left, partner, current)
        stacked = jnp.concatenate([left_part, right_part], axis=1)
        entry = (position >> height) * (1 << height) + (1 << height - 1)
        node_inv = lax.dynamic_slice_in_dim(every_inv, entry, 1, 0)
        node_basis = lax.dynamic_slice_in_dim(every_basis, entry, 1, 0)
        node_back = lax.dynamic_slice_in_dim(every_back, entry, 1, 0)
        node_coarse = lax.dynamic_slice_in_dim(every_coarse, entry, 1, 0)
        solved, reduced, current = node_up(node_inv, node_basis, node_coarse, stacked)
        stored.append((solved, reduced, node_back, is_left))
    parent_part = None
    for height in range(tree_depth, 0, -1):
        solved, reduced, node_back, is_left = stored[height - 1]
        if parent_part is None:
            halves = solved
        else:
            halves = node_down(solved, reduced, node_back, parent_part)
        parent_part = jnp.where(is_left, halves[:, :basis_rank], halves[:, basis_rank:])
    return parent_part


def per_device(
    rhs_cols,
    leaf_inv,
    leaf_basis,
    leaf_back,
    leaf_coarse,
    mid_inv,
    mid_basis,
    mid_back,
    mid_coarse,
    top_inv,
    top_basis,
    top_back,
    top_coarse,
):
    leaf_count = leaf_inv.shape[0]
    leaf_width = leaf_inv.shape[2]
    basis_rank = leaf_basis.shape[2]
    columns = rhs_cols.shape[1]
    blocks = rhs_cols.reshape(leaf_count, leaf_width, columns)
    leaf_vals = jnp.einsum(
        "nij,njc->nic",
        lax.all_gather(leaf_inv, "rhs", axis=1, tiled=True),
        blocks,
        preferred_element_type=jnp.float32,
    ).astype(jnp.bfloat16)
    leaf_proj = jnp.einsum(
        "nik,nic->nkc", leaf_basis, leaf_vals, preferred_element_type=jnp.float32
    )
    current = jnp.einsum("nkl,nlc->nkc", leaf_coarse, leaf_proj, precision=exact_mode)
    local_levels = leaf_count.bit_length() - 1
    stored = []
    for height in range(1, local_levels + 1):
        offset = leaf_count - (leaf_count >> height - 1)
        node_count = leaf_count >> height
        stacked = current.reshape(node_count, 2 * basis_rank, columns)
        solved, reduced, current = node_up(
            mid_inv[offset : offset + node_count],
            mid_basis[offset : offset + node_count],
            mid_coarse[offset : offset + node_count],
            stacked,
        )
        stored.append((solved, reduced, mid_back[offset : offset + node_count]))
    leaf_total = lax.axis_size("leaf")
    tree_depth = leaf_total.bit_length() - 1
    position = lax.axis_index("leaf")
    every_inv, every_basis, every_back, every_coarse = (
        lax.all_gather(top_inv, "leaf", axis=0, tiled=True),
        lax.all_gather(top_basis, "leaf", axis=0, tiled=True),
        lax.all_gather(top_back, "leaf", axis=0, tiled=True),
        lax.all_gather(top_coarse, "leaf", axis=0, tiled=True),
    )
    parent_part = top_doubling(
        current, every_inv, every_basis, every_back, every_coarse, tree_depth, position
    )
    for solved, reduced, back_part in reversed(stored):
        halves = node_down(solved, reduced, back_part, parent_part)
        parent_part = halves.reshape(2 * halves.shape[0], basis_rank, columns)
    difference = (leaf_proj - parent_part).astype(jnp.bfloat16)
    result = leaf_vals.astype(jnp.float32) - jnp.einsum(
        "nik,nkc->nic", leaf_back, difference, preferred_element_type=jnp.float32
    )
    return result.reshape(leaf_count * leaf_width, columns)


def solution(mesh):
    return jax.shard_map(
        per_device,
        mesh=mesh,
        in_specs=(
            P("leaf", "rhs"),
            P("leaf", "rhs", None),
            P("leaf", None, None),
            P("leaf", None, None),
            P("leaf", None, None),
            P("leaf", None, None),
            P("leaf", None, None),
            P("leaf", None, None),
            P("leaf", None, None),
            P("leaf", None, None),
            P("leaf", None, None),
            P("leaf", None, None),
            P("leaf", None, None),
        ),
        out_specs=P("leaf", "rhs"),
        check_vma=False,
    )
```

profile of v0, /device:TPU:0, one launch (start us, length us, event | category | flops | bytes accessed | tf_op | source)
XLA Modules:
  0.0 282.1 jit_solution(17705519736314220675)
XLA Ops:
  6.5 0.7 all-gather.5.cloned.1.call-update
  7.3 0.7 all-gather.7.cloned.1.call-update
  8.0 0.0 all-gather.11.cloned.1.call-start
  8.1 0.7 all-gather.11.cloned.1.call-update
  8.7 0.0 all-gather.9.cloned.1.call-start
  8.8 0.5 all-gather.9.cloned.1.call-update
  9.3 152.0 %all-gather.5.cloned.1.call-done = bf16[16,512,512]{2,1,0:T(8,128)(2,1)} async-done(((bf16[16,128,512]{2,1,0:T(8,128)(2,1)}), bf16[16,512,512]{2,1,0:T(8,128)(2,1)}) %all-gather.5.cloned.1.call-update) | async-done | bytes 8388624 | tf_op jit(solution)/shard_map/all_gather | solution.py:76
  161.3 5.9 %convolution_convert_fusion = bf16[16,512,128]{2,1,0:T(8,128)(2,1)S(1)} fusion(bf16[16,512,512]{2,1,0:T(8,128)(2,1)} %all-gather.5.cloned.1.call-done, bf16[16,512,128]{2,1,0:T(8,128)(2,1)S(1)} %bitcast.153), kind=kOutput, calls=%fused_computation.3 | convolution fusion | flops 1074790400 | bytes 12582912 | tf_op jit(solution)/shard_map/nij,njc->nic/dot_general | solution.py:74
  167.2 0.8 fusion.97
  168.0 0.5 copy-done.2
  168.5 0.7 copy-done.13
  169.2 2.3 fusion.98
  171.5 2.4 fusion
  174.0 1.2 fusion.12
  175.2 0.4 copy-done.14
  175.6 1.2 fusion.20
  176.8 1.3 fusion.10
  178.1 0.7 fusion.18
  178.8 0.7 fusion.36
  179.4 0.7 fusion.16
  180.2 0.4 fusion.34
  180.6 0.4 fusion.59
  181.0 0.4 fusion.27
  181.4 0.3 fusion.51
  181.7 0.4 copy-done.10
  182.1 0.3 convolution_bitcast_fusion.3
  182.3 0.1 collective-permute-start
  182.5 0.2 copy-done.15
  182.7 11.1 %all_gather.19 = f32[8,128,128]{2,1,0:T(8,128)} all-gather(f32[1,128,128]{2,1,0:T(8,128)S(1)} %copy-done.18), channel_id=1, replica_groups=mesh['leaf'=8,'rhs'=4] {'leaf'}, dimensions={0}, use_global_device_ids=true | all-gather | bytes 589824 | tf_op jit(solution)/shard_map/all_gather | solution.py:104
  193.8 0.6 broadcast_select_fusion.5
  194.4 1.4 fusion.25
  195.8 19.8 %all-gather.11.cloned.1.call-done = f32[8,256,128]{2,1,0:T(8,128)} async-done(((f32[1,256,128]{2,1,0:T(8,128)}), f32[8,256,128]{2,1,0:T(8,128)}) %all-gather.11.cloned.1.call-update) | async-done | bytes 1048592 | tf_op jit(solution)/shard_map/all_gather | solution.py:102
  215.6 1.3 fusion.48
  216.9 0.6 copy-done.16
  217.5 1.7 convolution_bitcast_fusion.2
  219.2 1.5 collective-permute-start.1
  220.7 3.1 %collective-permute-done.1 = f32[1,128,128]{2,1,0:T(8,128)} collective-permute-done((f32[1,128,128]{2,1,0:T(8,128)}, f32[1,128,128]{2,1,0:T(8,128)}, u32[]{:S(2)}, u32[]{:S(2)}) %collective-permute-start.1) | collective-permute-done | bytes 65568 | tf_op jit(solution)/shard_map/ppermute | solution.py:10
  223.8 0.9 broadcast_select_fusion.3
  224.7 1.3 fusion.23
  226.1 0.6 copy-done.9
  226.7 1.3 fusion.45
  228.0 0.6 copy-done.17
  228.6 1.7 convolution_bitcast_fusion.1
  230.3 1.4 collective-permute-start.2
  231.7 0.8 copy.43
  232.5 2.4 collective-permute-done.2
  234.9 0.9 broadcast_select_fusion.1
  235.8 2.0 convolution_bitcast_fusion
  237.7 3.2 %all-gather.9.cloned.1.call-done = f32[8,256,128]{2,1,0:T(8,128)} async-done(((f32[1,256,128]{2,1,0:T(8,128)}), f32[8,256,128]{2,1,0:T(8,128)}) %all-gather.9.cloned.1.call-update) | async-done | bytes 1048592 | tf_op jit(solution)/shard_map/all_gather | solution.py:103
  240.9 1.3 fusion.7
  242.2 1.3 fusion.6
  243.6 1.9 fusion.5
  245.5 1.6 copy.45
  247.2 1.7 copy.46
  248.8 2.2 fusion.4
  251.0 1.8 copy.47
  252.8 1.8 copy.48
  254.6 2.7 fusion.3
  257.2 2.0 copy.49
  259.3 2.0 copy.50
  261.3 3.9 %fusion.2 = f32[8,256,128]{1,2,0:T(8,128)} fusion(f32[8,128,256]{2,1,0:T(8,128)} %copy-done.1, f32[15,256,128]{2,1,0:T(8,128)} %param.20, f32[8,128,128]{1,2,0:T(8,128)} %copy.50, f32[8,128,128]{2,1,0:T(8,128)} %copy-done.3), kind=kOutput, calls=%fused_computation.5 | convolution fusion | flops 403046400 | bytes 4194304 | tf_op jit(solution)/shard_map/nik,nkc->nic/dot_general | solution.py:21
  265.2 2.5 copy.51
  267.7 2.5 copy.52
  270.3 5.3 %bitcast_subtract_fusion = f32[16,512,128]{2,1,0:T(8,128)} fusion(bf16[16,512,128]{2,1,0:T(8,128)(2,1)} %copy-done.2, bf16[16,512,128]{2,1,0:T(8,128)(2,1)} %param.16, f32[16,128,128]{1,2,0:T(8,128)} %copy.52, f32[16,128,128]{2,1,0:T(8,128)S(1)} %fusion.97), kind=kOutput, calls=%fused_computation | convolution fusion | flops 271056896 | bytes 10485760 | tf_op jit(solution)/shard_map/nik,nkc->nic/dot_general | solution.py:113
  (34 shorter events, 0.1 us)
Async XLA Ops:
  6.5 154.8 %copy-start = (bf16[8192,128]{1,0:T(8,128)(2,1)S(1)}, bf16[8192,128]{1,0:T(8,128)(2,1)}, u32[]{:S(2)}) copy-start(bf16[8192,128]{1,0:T(8,128)(2,1)} %param.13) | copy-start | bytes 6291460
  6.5 154.8 %all-gather.5.cloned.1.call-start = ((), (), s32[]{:S(2)}) async-start(), calls=%async_computation | async-start | bytes 10485760 | tf_op jit(solution)/shard_map/all_gather | solution.py:76
  7.3 187.1 %all-gather.7.cloned.1.call-start = ((), (), s32[]{:S(2)}) async-start(), calls=%async_computation.1 | async-start | bytes 2359296 | tf_op jit(solution)/shard_map/all_gather | solution.py:101
  8.0 207.6 %all-gather.11.cloned.1.call-start = ((), (), s32[]{:S(2)}) async-start(), calls=%async_computation.3 | async-start | bytes 1179648 | tf_op jit(solution)/shard_map/all_gather | solution.py:102
  8.7 232.1 %all-gather.9.cloned.1.call-start = ((), (), s32[]{:S(2)}) async-start(), calls=%async_computation.2 | async-start | bytes 1179648 | tf_op jit(solution)/shard_map/all_gather | solution.py:103
  161.3 5.9 %copy-start.7 = (bf16[16,512,128]{2,1,0:T(8,128)(2,1)S(1)}, bf16[16,512,128]{2,1,0:T(8,128)(2,1)}, u32[]{:S(2)}) copy-start(bf16[16,512,128]{2,1,0:T(8,128)(2,1)} %param.15) | copy-start | bytes 6291460
  167.2 1.3 copy-start.2
  167.2 2.0 copy-start.13
  167.2 4.3 %copy-start.5 = (f32[15,256,256]{2,1,0:T(8,128)S(1)}, f32[15,256,256]{2,1,0:T(8,128)}, u32[]{:S(2)}) copy-start(f32[15,256,256]{2,1,0:T(8,128)} %param.18) | copy-start | bytes 11796484
  171.5 2.5 copy-start.8
  174.0 2.8 copy-start.1
  174.0 1.6 copy-start.14
  175.6 3.2 %copy-start.3 = (f32[8,128,128]{2,1,0:T(8,128)}, f32[8,128,128]{2,1,0:T(8,128)S(1)}, u32[]{:S(2)}) copy-start(f32[8,128,128]{2,1,0:T(8,128)S(1)} %fusion.12) | copy-start | bytes 1572868
  178.1 2.9 %copy-start.4 = (f32[4,128,256]{2,1,0:T(8,128)}, f32[4,128,256]{2,1,0:T(8,128)S(1)}, u32[]{:S(2)}) copy-start(f32[4,128,256]{2,1,0:T(8,128)S(1)} %fusion.10) | copy-start | bytes 1572868
  178.8 3.9 %copy-start.18 = (f32[1,128,128]{2,1,0:T(8,128)S(1)}, f32[1,128,128]{2,1,0:T(8,128)}, u32[]{:S(2)}) copy-start(f32[1,128,128]{2,1,0:T(8,128)} %param.25) | copy-start | bytes 196612
  180.2 1.2 copy-start.6
  180.6 1.8 copy-start.11
  181.4 0.7 copy-start.10
  182.1 0.6 copy-start.15
  182.3 11.4 %collective-permute-start = (f32[1,128,128]{1,2,0:T(8,128)S(1)}, f32[1,128,128]{1,2,0:T(8,128)S(1)}, u32[]{:S(2)}, u32[]{:S(2)}) collective-permute-start(f32[1,128,128]{1,2,0:T(8,128)S(1)} %convolution_bitcast_fusion.3), channel_id=1, source_target_pairs={{0,4},{4,0},{8,12},{12,8},{16,20},{20,16},{24,28},{28,24},{1,5},{5... | collective-permute-start | bytes 196616 | tf_op jit(solution)/shard_map/ppermute | solution.py:10
  216.9 0.6 copy-start.16
  219.2 4.6 %collective-permute-start.1 = (f32[1,128,128]{2,1,0:T(8,128)}, f32[1,128,128]{2,1,0:T(8,128)}, u32[]{:S(2)}, u32[]{:S(2)}) collective-permute-start(f32[1,128,128]{2,1,0:T(8,128)} %convolution_bitcast_fusion.2), channel_id=1, source_target_pairs={{0,8},{4,12},{8,0},{12,4},{16,24},{20,28},{24,16},{28,20},{1,9},{5... | collective-permute-start | bytes 196616 | tf_op jit(solution)/shard_map/ppermute | solution.py:10
  226.1 0.6 copy-start.9
  228.0 0.6 copy-start.17
  230.3 4.6 %collective-permute-start.2 = (f32[1,128,128]{2,1,0:T(8,128)}, f32[1,128,128]{2,1,0:T(8,128)}, u32[]{:S(2)}, u32[]{:S(2)}) collective-permute-start(f32[1,128,128]{2,1,0:T(8,128)} %convolution_bitcast_fusion.1), channel_id=1, source_target_pairs={{0,16},{4,20},{8,24},{12,28},{16,0},{20,4},{24,8},{28,12},{1,17},{... | collective-permute-start | bytes 196616 | tf_op jit(solution)/shard_map/ppermute | solution.py:10
  232.5 16.4 %copy-start.12 = (f32[2,128,128]{2,1,0:T(8,128)S(1)}, f32[2,128,128]{2,1,0:T(8,128)}, u32[]{:S(2)}) copy-start(f32[2,128,128]{2,1,0:T(8,128)} %copy-done.11) | copy-start | bytes 393220
Sparse Core Ops, SparseCore 0:
  8.9 152.3 all-gather.4
  163.2 26.0 all-gather.6
  191.2 24.3 all-gather.10
  217.4 23.4 all-gather.8
where the time goes:
time: 283 us; the launch traced here: 282 us
  waiting for transfers between devices  183 us (65%)
  matrix products  48 us (17%)
  local copies, waits for them, and re-layouts  20.9 us (7%)
  between operations  13.5 us (5%)
  blocking collectives  11.1 us (4%)
  starting transfers between devices  3.12 us (1%)
    all_gather x1, waiting for transfers between devices, per_device(): lax.all_gather(leaf_inv, 'rhs', axis=1, tiled=True)  152 us
    all_gather x1, waiting for transfers between devices, per_device(): lax.all_gather(top_basis, 'leaf', axis=0, tiled=True)  19.8 us
    dot_general x6, matrix products, node_down(): jnp.einsum('nik,nkc->nic', back_mat, reduced - parent_part, precision=exa...  13.3 us
    all_gather x1, blocking collectives, per_device(): lax.all_gather(top_coarse, 'leaf', axis=0, tiled=True)  11.1 us
    dot_general x7, matrix products, node_up(): solved = jnp.einsum('nij,njc->nic', inverse, stacked, precision=exact_mode)  9.52 us
    reshape x4, local copies, waits for them, and re-layouts, per_device(): parent_part = halves.reshape(2 * halves.shape[0], basis_rank, columns)  8.04 us
    sub x4, local copies, waits for them, and re-layouts, node_down(): solved - jnp.einsum('nik,nkc->nic', back_mat, reduced - parent_part, prec...  7.99 us
    dot_general x6, matrix products, node_up(): upward = jnp.einsum('nkl,nlc->nkc', coarse, reduced, precision=exact_mode)  5.88 us
  transfers between devices with their start and end apart: 7, of which 5 were waited for; matrix products, arithmetic and copies ran while one was open for 12% of the time, Pallas kernels for 0%

commit v1 on v0

v1 whole, which is shorter than its diff:
```python
import functools

import jax
import jax.numpy as jnp
from jax import lax
from jax.experimental import pallas as pl
from jax.experimental.pallas import tpu as pltpu
from jax.sharding import PartitionSpec as P

MESH = pl.DeviceIdType.MESH
f32, bf16 = jnp.float32, jnp.bfloat16
OWN_AHEAD, END_AHEAD, INNER_LAG, END_LAG = 4, 2, 2, 5


def split(a):
    high = a.astype(bf16)
    return high, (a - high.astype(f32)).astype(bf16)


def dot3(a, b, dims=(((1,), (0,)), ((), ()))):
    (ah, al), (bh, bl) = split(a), split(b)
    dot = functools.partial(lax.dot_general, dimension_numbers=dims, preferred_element_type=f32)
    return dot(ah, bh) + (dot(al, bh) + dot(ah, bl))


TRANSPOSED = (((0,), (0,)), ((), ()))


def tree_kernel(leaf_total, rhs, inv, basis, coarse, mid_inv, mid_basis, mid_back, mid_coarse,
                top_inv, top_basis, top_back, top_coarse, vals_out, diff_out,
                inv_v, rhs_v, rhs_far, vals, vals_far, basis_v, coarse_v, mi, mb, mk, mc, ti, tb, tk, tc,
                mid_g, mid_f, gs, acc, proj, zs, top_m, top_w, top_a, top_g, top_in,
                load, inv_s, inv_end_r, inv_mid_r, fwd_s, fwd_r, rhs_s, rhs_r, res_s, res_r,
                out_s, top_s, top_r, ex_s, ex_r):
    leaves, rows, width = inv.shape
    rank, cols = basis.shape[2], rhs.shape[2]
    levels = leaves.bit_length() - 1
    depth = leaf_total.bit_length() - 1
    pos, z = lax.axis_index("leaf"), lax.axis_index("rhs")
    inner = (z == 1) | (z == 2)
    end = jnp.logical_not(inner)
    low = z < 2
    end_z = jnp.where(low, 0, 3)
    mid_z = jnp.where(low, 1, 2)
    pair_z = jnp.where(low, 2, 1)
    pair_end = jnp.where(low, 3, 0)

    def slot(l, who):
        return inv_v.at[l, pl.ds(pl.multiple_of(who * rows, rows), rows), :]

    def remote(src, dst, s, r, where):
        return pltpu.make_async_remote_copy(src_ref=src, dst_ref=dst, send_sem=s, recv_sem=r,
                                            device_id=where, device_id_type=MESH)

    def inv_to_mid(l):
        return remote(inv.at[l], slot(l, end_z), inv_s.at[l], inv_end_r.at[l], {"rhs": mid_z})

    def inv_to_pair(l):
        return remote(inv.at[l], slot(l, z), inv_s.at[l], inv_mid_r.at[l], {"rhs": pair_z})

    def forward(l):
        return remote(slot(l, end_z), slot(l, end_z), fwd_s.at[l], fwd_r.at[l], {"rhs": pair_z})

    def rhs_to_mid(l):
        return remote(rhs.at[l], rhs_far.at[l], rhs_s.at[l], rhs_r.at[l], {"rhs": mid_z})

    def result(l):
        return remote(vals_far.at[l], vals.at[l], res_s.at[l], res_r.at[l], {"rhs": end_z})

    def vals_copy(l):
        return pltpu.make_async_copy(vals.at[l], vals_out.at[l], out_s.at[l])

    pairs = [(basis, basis_v), (coarse, coarse_v), (mid_inv, mi), (mid_basis, mb), (mid_back, mk),
             (mid_coarse, mc), (top_inv, ti), (top_basis, tb), (top_back, tk), (top_coarse, tc)]
    loads = [pltpu.make_async_copy(a, b, load.at[i]) for i, (a, b) in enumerate(pairs)]
    own_inv = pltpu.make_async_copy(
        inv, inv_v.at[:, pl.ds(pl.multiple_of(z * rows, rows), rows), :], load.at[len(pairs)])
    own_rhs = pltpu.make_async_copy(rhs, rhs_v, load.at[len(pairs) + 1])

    barrier = pltpu.get_barrier_semaphore()

    def greet(k, carry):
        pl.semaphore_signal(barrier, inc=1, device_id={"leaf": lax.rem(pos + k, leaf_total)}, device_id_type=MESH)
        return carry

    lax.fori_loop(1, leaf_total, greet, 0)

    @pl.when(inner)
    def _():
        pl.semaphore_signal(barrier, inc=1, device_id={"rhs": end_z}, device_id_type=MESH)
        pl.semaphore_signal(barrier, inc=1, device_id={"rhs": pair_z}, device_id_type=MESH)
        pl.semaphore_wait(barrier, leaf_total + 1)

    @pl.when(end)
    def _():
        pl.semaphore_signal(barrier, inc=1, device_id={"rhs": mid_z}, device_id_type=MESH)
        pl.semaphore_wait(barrier, leaf_total)

    @pl.when(inner)
    def _():
        def go(l, carry):
            inv_to_pair(l).start()
            return carry

        lax.fori_loop(0, min(OWN_AHEAD, leaves), go, 0)
        own_inv.start()
        own_rhs.start()

    @pl.when(end)
    def _():
        def go(l, carry):
            inv_to_mid(l).start()
            rhs_to_mid(l).start()
            return carry

        lax.fori_loop(0, min(END_AHEAD, leaves), go, 0)

    for copy in loads:
        copy.start()
    for copy in loads:
        copy.wait()

    @pl.when(inner)
    def _():
        own_inv.wait()
        own_rhs.wait()

    def merge(e, u, w, s):
        reduced = dot3(u, e, TRANSPOSED)
        return dot3(s, reduced), e - dot3(w, reduced)

    def top_copies(height, k):
        base = (pos // (1 << height)) * (1 << height)
        target = base + lax.rem(pos - base + k, 1 << height)
        i = height - 1
        return (remote(top_m.at[i], top_m.at[i], top_s.at[0, k], top_r.at[0, i], {"leaf": target}),
                remote(top_w.at[i], top_w.at[i], top_s.at[1, k], top_r.at[1, i], {"leaf": target}))

    for height in range(1, depth + 1):
        @pl.when(lax.rem(pos, 1 << height) == 1 << (height - 1))
        def _():
            top_w[height - 1] = tk[0]
            g_mat, f_mat = merge(ti[0], tb[0], tk[0], tc[0])
            top_m[height - 1, 0:rank, :] = g_mat
            top_m[height - 1, rank:, :] = ti[0] if height == depth else f_mat

            def go(k, carry):
                for copy in top_copies(height, k):
                    copy.start()
                return carry

            lax.fori_loop(1, 1 << height, go, 0)

    def first(height):
        return 2 * leaves - (2 * leaves >> height)

    def pair_of(height, p):
        i = first(height - 1) + 2 * p
        return jnp.concatenate([gs[i], gs[i + 1]], axis=0)

    def visits(l, body):
        for height in range(1, levels + 1):
            @pl.when(lax.rem(l + 1, 1 << height) == 0)
            def _():
                p = (l + 1) // (1 << height) - 1
                body(height, p, first(height) - leaves + p)

    def prepare(height, p, row):
        mid_g[row], mid_f[row] = merge(mi[row], mb[row], mk[row], mc[row])

    def upward(height, p, row):
        gs[first(height) + p] = dot3(mid_g[row], pair_of(height, p))

    def aside(height, p, row):
        acc[row] = dot3(mid_f[row], pair_of(height, p))

    lag = jnp.where(inner, INNER_LAG, END_LAG)

    def step(t, carry):
        @pl.when((t < leaves) & inner)
        def _():
            inv_end_recv = remote(inv.at[t], slot(t, end_z), inv_s.at[t], inv_end_r.at[t], {"rhs": end_z})
            inv_end_recv.wait_recv()
            forward(t).start()
            inv_to_pair(t).wait_send()

            @pl.when(t + OWN_AHEAD < leaves)
            def _():
                inv_to_pair(t + OWN_AHEAD).start()

        @pl.when((t < leaves) & end)
        def _():
            inv_to_mid(t).wait_send()
            rhs_to_mid(t).wait_send()

            @pl.when(t + END_AHEAD < leaves)
            def _():
                inv_to_mid(t + END_AHEAD).start()
                rhs_to_mid(t + END_AHEAD).start()

        l = t - lag

        @pl.when((l >= 0) & (l < leaves))
        def _():
            visits(l, prepare)

            @pl.when(inner)
            def _():
                remote(inv.at[l], slot(l, pair_z), inv_s.at[l], inv_mid_r.at[l], {"rhs": pair_z}).wait_recv()
                remote(slot(l, end_z), slot(l, pair_end), fwd_s.at[l], fwd_r.at[l], {"rhs": pair_z}).wait_recv()
                remote(rhs.at[l], rhs_far.at[l], rhs_s.at[l], rhs_r.at[l], {"rhs": end_z}).wait_recv()
                both = jnp.concatenate([rhs_v[l], rhs_far[l]], axis=1)
                solved = jnp.dot(inv_v[l], both, preferred_element_type=f32).astype(bf16)
                vals_far[l] = solved[:, cols:]
                result(l).start()
                vals[l] = solved[:, :cols]

            @pl.when(end)
            def _():
                remote(vals_far.at[l], vals.at[l], res_s.at[l], res_r.at[l], {"rhs": mid_z}).wait_recv()

            vals_copy(l).start()
            mine = lax.dot_general(basis_v[l], vals[l], TRANSPOSED, preferred_element_type=f32)
            proj[l] = mine
            gs[l] = dot3(coarse_v[l], mine)
            visits(l, upward)

            @pl.when(l < leaves - 1)
            def _():
                visits(l, aside)

        return carry

    lax.fori_loop(0, leaves + END_LAG, step, 0)

    def exchange(height):
        partner = pos + jnp.where(lax.rem(pos // (1 << (height - 1)), 2) == 0, 1, -1) * (1 << (height - 1))
        return remote(top_g.at[height - 1], top_in.at[height - 1], ex_s.at[height - 1], ex_r.at[height - 1],
                      {"leaf": partner})

    top_g[0] = gs[first(levels)]
    side = [lax.rem(pos // (1 << (height - 1)), 2) for height in range(1, depth + 1)]

    def stacked(height):
        i = height - 1
        left = side[i] == 0
        return jnp.concatenate([jnp.where(left, top_g[i], top_in[i]), jnp.where(left, top_in[i], top_g[i])], axis=0)

    def half(height):
        return pl.ds(pl.multiple_of(side[height - 1] * rank, rank), rank)

    def top_aside(height):
        i = height - 1
        lower = pl.ds(pl.multiple_of((side[i] + 1) * rank, rank), rank)
        top_a[i] = dot3(top_m[i, lower, :], stacked(height))

    for height in range(1, depth + 1):
        i = height - 1
        exchange(height).start()
        if height == 1:
            visits(leaves - 1 + jnp.int32(0), aside)
        else:
            top_aside(height - 1)

        @pl.when(lax.rem(pos, 1 << height) != 1 << i)
        def _():
            for copy in top_copies(height, 1):
                copy.wait_recv()

        exchange(height).wait_recv()
        if height < depth:
            top_g[height] = dot3(top_m[i, 0:rank, :], stacked(height))
    top_aside(depth)
    down = top_a[depth - 1]
    for height in range(depth - 1, 0, -1):
        i = height - 1
        down = top_a[i] + dot3(top_w[i, half(height), :], down)
    zs[first(levels)] = down

    for height in range(levels, 0, -1):
        def lower(p, carry):
            row = first(height) - leaves + p
            halves = acc[row] + dot3(mk[row], zs[first(height) + p])
            for j in range(2):
                part = halves[j * rank:(j + 1) * rank]
                if height > 1:
                    zs[first(height - 1) + 2 * p + j] = part
                else:
                    diff_out[2 * p + j] = (proj[2 * p + j] - part).astype(bf16)
            return carry

        lax.fori_loop(0, leaves >> height, lower, 0)

    for height in range(1, depth + 1):
        exchange(height).wait_send()

        @pl.when(lax.rem(pos, 1 << height) == 1 << (height - 1))
        def _():
            def done(k, carry):
                for copy in top_copies(height, k):
                    copy.wait_send()
                return carry

            lax.fori_loop(1, 1 << height, done, 0)

    def finish(l, carry):
        vals_copy(l).wait()

        @pl.when(inner)
        def _():
            forward(l).wait_send()
            result(l).wait_send()

        return carry

    lax.fori_loop(0, leaves, finish, 0)


def output_kernel(vals, back, diff, out):
    out[0] = vals[0].astype(f32) - jnp.dot(back[0], diff[0], preferred_element_type=f32)


def per_device(leaf_total, rhs_cols, leaf_inv, leaf_basis, leaf_back, leaf_coarse, mid_inv, mid_basis,
               mid_back, mid_coarse, top_inv, top_basis, top_back, top_coarse):
    leaves, rows, width = leaf_inv.shape
    rank, cols = leaf_basis.shape[2], rhs_cols.shape[1]
    depth = leaf_total.bit_length() - 1
    blocks = rhs_cols.reshape(leaves, width, cols)
    dma = pltpu.SemaphoreType.DMA
    mids = mid_inv.shape[0]
    operands = (blocks, leaf_inv, leaf_basis, leaf_coarse, mid_inv, mid_basis, mid_back, mid_coarse,
                top_inv, top_basis, top_back, top_coarse)
    small = [pltpu.VMEM(a.shape, a.dtype) for a in operands[2:]]
    vals, diff = pl.pallas_call(
        functools.partial(tree_kernel, leaf_total),
        out_shape=(jax.ShapeDtypeStruct((leaves, width, cols), bf16),
                   jax.ShapeDtypeStruct((leaves, rank, cols), bf16)),
        in_specs=[pl.BlockSpec(memory_space=pl.ANY)] * len(operands),
        out_specs=(pl.BlockSpec(memory_space=pl.ANY), pl.BlockSpec(memory_space=pltpu.VMEM)),
        scratch_shapes=[
            pltpu.VMEM((leaves, width, width), bf16),
            pltpu.VMEM((leaves, width, cols), bf16),
            pltpu.VMEM((leaves, width, cols), bf16),
            pltpu.VMEM((leaves, width, cols), bf16),
            pltpu.VMEM((leaves, width, cols), bf16),
            *small,
            pltpu.VMEM((mids, rank, 2 * rank), f32),
            pltpu.VMEM((mids, 2 * rank, 2 * rank), f32),
            pltpu.VMEM((2 * leaves, rank, cols), f32),
            pltpu.VMEM((mids, 2 * rank, cols), f32),
            pltpu.VMEM((leaves, rank, cols), f32),
            pltpu.VMEM((2 * leaves, rank, cols), f32),
            pltpu.VMEM((depth, 3 * rank, 2 * rank), f32),
            pltpu.VMEM((depth, 2 * rank, rank), f32),
            pltpu.VMEM((depth, rank, cols), f32),
            pltpu.VMEM((depth, rank, cols), f32),
            pltpu.VMEM((depth, rank, cols), f32),
            dma((len(operands),)),
            *[dma((leaves,)) for _ in range(10)],
            dma((2, leaf_total)),
            dma((2, depth)),
            dma((depth,)),
            dma((depth,)),
        ],
        compiler_params=pltpu.CompilerParams(
            collective_id=0, has_side_effects=True, vmem_limit_bytes=56 * 1024 * 1024),
    )(*operands)

    def block(*shape):
        return pl.BlockSpec((1,) + shape, lambda i: (i, 0, 0))

    result = pl.pallas_call(
        output_kernel,
        grid=(leaves,),
        out_shape=jax.ShapeDtypeStruct((leaves, width, cols), f32),
        in_specs=[block(width, cols), block(width, rank), block(rank, cols)],
        out_specs=block(width, cols),
    )(vals, leaf_back, diff)
    return result.reshape(leaves * width, cols)


def solution(mesh):
    shards = P("leaf", None, None)
    return jax.shard_map(
        functools.partial(per_device, mesh.shape["leaf"]),
        mesh=mesh,
        in_specs=(P("leaf", "rhs"), P("leaf", "rhs", None)) + (shards,) * 11,
        out_specs=P("leaf", "rhs"),
        check_vma=False,
    )
```

time: 283 us -> 132 us (0.47)
  waiting for transfers between devices: 183 us -> 0 us
  Pallas kernels: 0 us -> 132 us
  matrix products: 48 us -> 0 us
  local copies, waits for them, and re-layouts: 20.9 us -> 0 us
  between operations: 13.5 us -> 0.01 us
  blocking collectives: 11.1 us -> 0 us
  starting transfers between devices: 3.12 us -> 0 us
    all_gather x4 -> x0, waiting for transfers between devices: 175 us -> none  [the longest x1 152 us: per_device(): lax.all_gather(leaf_inv, 'rhs', axis=1, tiled=True)]
    pallas_call x0 -> x2, Pallas kernels: none -> 132 us  [the longest x1 120 us: per_device(): pl.pallas_call(functools.partial(tree_kernel, leaf_total), out_shape=(jax...]
    dot_general x29 -> x0, matrix products: 48 us -> none  [the longest x6 13.3 us: node_down(): jnp.einsum('nik,nkc->nic', back_mat, reduced - parent_part, precision=exa...]
    all_gather x1 -> x0, blocking collectives: 11.1 us -> none  [per_device(): lax.all_gather(top_coarse, 'leaf', axis=0, tiled=True)]
    reshape x4 -> x0, local copies, waits for them, and re-layouts: 8.04 us -> none  [per_device(): parent_part = halves.reshape(2 * halves.shape[0], basis_rank, columns)]
    sub x4 -> x0, local copies, waits for them, and re-layouts: 7.99 us -> none  [node_down(): solved - jnp.einsum('nik,nkc->nic', back_mat, reduced - parent_part, prec...]
    ppermute x3 -> x0, waiting for transfers between devices: 5.52 us -> none  [swapped(): lax.ppermute(array, axis, [(i, i ^ 1 << bit) for i in range(lax.axis_size...]
    unnamed x38 -> x0, local copies, waits for them, and re-layouts: 4.16 us -> none
  transfers between devices with their start and end apart: 7 -> 0, of which waited for: 5 -> 0; matrix products, arithmetic and copies ran while one was open for 12% -> 0% of each run, Pallas kernels for 0% -> 0%
where the time goes in v1:
time: 132 us
  Pallas kernels  132 us (100%)
    pallas_call x1, Pallas kernels, per_device(): pl.pallas_call(functools.partial(tree_kernel, leaf_total), out_shape=(jax...  120 us
    pallas_call x1, Pallas kernels, per_device(): pl.pallas_call(output_kernel, grid=(leaves,), out_shape=jax.ShapeDtypeStr...  11.4 us

profile of v1, /device:TPU:0, one launch (start us, length us, event | category | flops | bytes accessed | tf_op | source)
XLA Modules:
  0.0 131.6 jit_solution(16987822386325665037)
XLA Ops:
  0.0 120.2 %shard_map.127 = (bf16[16,512,128]{2,1,0:T(8,128)(2,1)}, bf16[16,128,128]{2,1,0:T(8,128)(2,1)}) custom-call(bf16[16,512,128]{2,1,0:T(8,128)(2,1)} %bitcast.2, bf16[16,128,512]{2,1,0:T(8,128)(2,1)} %inv.1, bf16[16,512,128]{2,1,0:T(8,128)(2,1)} %basis.1, f32[16,128,128]{2,1,0:T(8,128)} %coarse.1, f32[15,256,256]{2,1,0:T(8,128)} %mid_inv.1, ...), custom_call_target="tpu_custom_call" | custom-call | tf_op jit(solution)/shard_map/pallas_call | solution.py:334
  120.2 11.4 %shard_map.128 = f32[16,512,128]{2,1,0:T(8,128)} custom-call(bf16[16,512,128]{2,1,0:T(8,128)(2,1)} %get-tuple-element.7.vals, bf16[16,512,128]{2,1,0:T(8,128)(2,1)} %back.1, bf16[16,128,128]{2,1,0:T(8,128)(2,1)} %get-tuple-element.8.diff), custom_call_target="tpu_custom_call" | custom-call | tf_op jit(solution)/shard_map/pallas_call | solution.py:372
